TPU v7x, 32 devices: a whole 2x2x4 slice. The times are simulated.
32 devices in a mesh: tm: 16 (over z, y, x), chan: 2 (over core).
Axes of the slice: x: 2, y: 2, z: 4, core: 2. Of those that a mesh axis runs over, the one named last changes fastest.
Arguments:
- latents: bfloat16 [96, 32, 896], P('chan', 'tm'), may hold values from -6 to 6
- weight: bfloat16 [27, 96, 96], replicated, may hold values from -0.125 to 0.125
- conv_bias: bfloat16 [96], P('chan'), may hold values from -3 to 3
- cotangent: bfloat16 [96, 32, 896], P('chan', 'tm'), may hold values from -6 to 6
Outputs:
- output: bfloat16 [96, 32, 896], P('chan', 'tm')
- grad_input: bfloat16 [96, 32, 896], P('chan', 'tm')
- grad_weight: float32 [27, 96, 96], P(None, 'chan')
- grad_bias: float32 [96], P('chan')
All inputs are finite; a program needn't handle non-finite values.
Results may differ from a plain program's by a relative error of at most 0.0085.
Values may be sent and summed in bfloat16 or wider, within the bound.
A program may use at most 64 MiB of HBM per device.

v0:
```python
import math

import jax
import jax.numpy as jnp
from jax import lax
from jax.sharding import PartitionSpec as P

HGT = 8
WID = 112


def shifted_2(value, axis, steps):
    count = lax.axis_size(axis)
    first, last = (max(0, -steps), min(count, count - steps))
    return lax.ppermute(value, axis, [(source, source + steps) for source in range(first, last)])


def shift_grid(volume, row_off, col_off):
    frames, channels, pixels = volume.shape
    grid_view = volume.reshape(frames, channels, HGT, WID)
    padded = jnp.pad(grid_view, ((0, 0), (0, 0), (1, 1), (1, 1)))
    return padded[:, :, row_off : row_off + HGT, col_off : col_off + WID].reshape(
        frames, channels, pixels
    )


def tap_stack(volume, inverse):
    frames, channels, pixels = volume.shape
    layers = []
    for row_tap in range(3):
        for col_tap in range(3):
            if inverse:
                layers.append(shift_grid(volume, 2 - row_tap, 2 - col_tap))
            else:
                layers.append(shift_grid(volume, row_tap, col_tap))
    return jnp.stack(layers, 1).reshape(frames, 9 * channels, pixels)


def kernel_block(weight, time_tap, out_start, out_amount, in_start, in_amount):
    return lax.dynamic_slice(
        weight, (time_tap * 9, out_start, in_start), (9, out_amount, in_amount)
    )


def forward_kernel(weight, time_tap, out_start, out_amount, in_start, in_amount):
    block = kernel_block(weight, time_tap, out_start, out_amount, in_start, in_amount)
    return block.transpose(1, 0, 2).reshape(out_amount, 9 * in_amount)


def input_kernel(weight, time_tap, out_start, out_amount, in_start, in_amount):
    block = kernel_block(weight, time_tap, out_start, out_amount, in_start, in_amount)
    return block.transpose(2, 0, 1).reshape(in_amount, 9 * out_amount)


def time_taps(kernels, stacked, frames, backward):
    running = None
    for time_tap in range(3):
        first_frame = 2 - time_tap if backward else time_tap
        partial_value = jnp.einsum(
            "ok,fkp->ofp",
            kernels[time_tap],
            stacked[first_frame : first_frame + frames],
            preferred_element_type=jnp.float32,
        )
        running = partial_value if time_tap == 0 else running + partial_value
    return running


def earlier_frames(volume):
    return shifted_2(volume, "tm", 1)


def later_frames(volume):
    return shifted_2(volume, "tm", -1)


def by_channels(latents, weight, conv_bias, cotangent):
    own_ch, frames, pixels = latents.shape
    full_ch = weight.shape[1]
    chan_start = lax.axis_index("chan") * own_ch
    tm_count = lax.axis_size("tm")
    earlier = earlier_frames(latents)
    extended = jnp.concatenate([earlier, latents], 1).transpose(1, 0, 2)
    inputs_stack = tap_stack(extended, False)
    offset = jnp.int32(0)
    amount = own_ch * lax.axis_size("chan")
    kernels = [
        forward_kernel(weight, time_tap, offset, amount, chan_start, own_ch)
        for time_tap in range(3)
    ]
    pre_act = lax.psum_scatter(
        time_taps(kernels, inputs_stack, frames, False), "chan", scatter_dimension=0, tiled=True
    )
    pre_act = pre_act + conv_bias.astype(jnp.float32)[:, None, None]
    sigmoid_pre = jax.nn.sigmoid(pre_act)
    output = (pre_act * sigmoid_pre).astype(jnp.bfloat16)
    grad_pre = (
        cotangent.astype(jnp.float32) * sigmoid_pre * (1.0 + pre_act * (1.0 - sigmoid_pre))
    ).astype(jnp.bfloat16)
    later_grads = later_frames(grad_pre)
    grads_ext = jnp.concatenate([grad_pre, later_grads], 1).transpose(1, 0, 2)
    grad_stack = tap_stack(grads_ext, True)
    offset = jnp.int32(0)
    amount = own_ch * lax.axis_size("chan")
    kernels = [
        input_kernel(weight, time_tap, chan_start, own_ch, offset, amount) for time_tap in range(3)
    ]
    grad_input = lax.psum_scatter(
        time_taps(kernels, grad_stack, frames, True), "chan", scatter_dimension=0, tiled=True
    )
    own_grads = grad_stack[:frames]
    shard_rows = lax.all_gather(extended, "chan", axis=1, tiled=True)
    width_now = shard_rows.shape[1]
    shifted = jnp.concatenate(
        [shard_rows[time_tap : time_tap + frames] for time_tap in range(3)], 1
    )
    product = jnp.einsum("fkp,fcp->kc", own_grads, shifted, preferred_element_type=jnp.float32)
    product = product.reshape(9 * own_ch, 3, width_now).transpose(1, 0, 2)
    norm_scale = 1.0 / math.sqrt(frames * tm_count * pixels)
    local_weight = product.reshape(27, own_ch, full_ch) * norm_scale
    local_bias = jnp.sum(grad_pre.astype(jnp.float32), axis=(1, 2)) * norm_scale
    grad_weight, grad_bias = lax.psum((local_weight, local_bias), "tm")
    return (output, grad_input.astype(jnp.bfloat16), grad_weight, grad_bias)


def local(latents, weight, conv_bias, cotangent):
    results = by_channels(latents, weight, conv_bias, cotangent)
    return results


def solution(mesh):
    in_specs = (P("chan", "tm", None), P(), P("chan"), P("chan", "tm", None))
    out_specs = (P("chan", "tm", None), P("chan", "tm", None), P(None, "chan", None), P("chan"))
    return jax.shard_map(local, mesh=mesh, in_specs=in_specs, out_specs=out_specs, check_vma=False)
```

profile of v0, /device:TPU:0, one launch (start us, length us, event | category | flops | bytes accessed | tf_op | source)
XLA Modules:
  0.0 229.8 jit_solution(8746487763678400545)
XLA Ops:
  7.2 1.0 copy.21
  8.2 4.9 %collective-permute-start = (bf16[48,2,896]{2,0,1:T(8,128)(2,1)S(1)}, bf16[48,2,896]{2,0,1:T(8,128)(2,1)S(1)}, u32[]{:S(2)}, u32[]{:S(2)}) collective-permute-start(bf16[48,2,896]{2,0,1:T(8,128)(2,1)S(1)} %copy.21), channel_id=1, source_target_pairs={{0,2},{2,4},{4,6},{6,8},{8,10},{10,12},{12,14},{14,16},{16,18},{18... | collective-permute-start | bytes 516104 | tf_op jit(solution)/shard_map/ppermute | solution.py:15
  13.1 1.4 constant_dynamic-slice_fusion
  17.2 2.2 pad_slice_fusion.8
  19.4 1.1 stack_reshape.54
  20.5 1.0 constant_dynamic-update-slice_fusion.9
  21.5 2.1 stack_reshape.55
  23.6 2.1 stack_reshape.56
  25.6 2.1 stack_reshape.57
  27.7 1.0 constant_dynamic-update-slice_fusion.8
  28.7 1.0 constant_dynamic-update-slice_fusion.7
  29.8 1.0 constant_dynamic-update-slice_fusion.6
  30.8 2.1 stack_reshape.59
  32.9 2.1 stack_reshape.60
  35.0 2.1 stack_reshape.61
  37.1 2.1 stack_reshape.62
  39.2 1.0 constant_dynamic-update-slice_fusion.5
  40.2 1.0 constant_dynamic-update-slice_fusion.4
  41.2 1.0 constant_dynamic-update-slice_fusion.3
  42.3 1.1 constant_dynamic-update-slice_fusion.2
  44.2 1.3 fusion.31
  45.5 10.5 %reduce-scatter.3.cloned.1.call-done = f32[48,2,896]{2,0,1:T(8,128)} async-done(((f32[96,2,896]{2,0,1:T(8,128)}), f32[48,2,896]{2,0,1:T(8,128)}) %reduce-scatter.3.cloned.1.call-update) | async-done | bytes 344080 | tf_op jit(solution)/shard_map/reduce_scatter | solution.py:91
  56.0 2.0 convert_reduce_fusion
  58.0 1.3 collective-permute-start.1
  59.3 7.2 %collective-permute-done.1 = bf16[48,2,896]{2,0,1:T(8,128)(2,1)S(1)} collective-permute-done((bf16[48,2,896]{2,0,1:T(8,128)(2,1)S(1)}, bf16[48,2,896]{2,0,1:T(8,128)(2,1)S(1)}, u32[]{:S(2)}, u32[]{:S(2)}) %collective-permute-start.1) | collective-permute-done | bytes 172064 | tf_op jit(solution)/shard_map/ppermute | solution.py:15
  67.7 2.2 pad_slice_fusion
  69.9 1.1 stack_reshape.63
  71.0 1.0 constant_dynamic-update-slice_fusion.17
  72.0 2.1 stack_reshape.64
  74.1 2.1 stack_reshape.65
  76.1 2.1 stack_reshape.66
  78.2 2.1 stack_reshape.68
  80.3 2.1 stack_reshape.69
  82.4 2.1 stack_reshape.70
  84.5 2.1 stack_reshape.71
  86.6 1.1 constant_dynamic-update-slice_fusion.16
  87.7 1.0 constant_dynamic-update-slice_fusion.15
  88.8 1.0 constant_dynamic-update-slice_fusion.14
  89.8 1.0 bitcast_dynamic-update-slice_fusion
  90.8 1.0 constant_dynamic-update-slice_fusion.13
  92.8 1.3 fusion.28
  94.2 2.3 %all_gather.3 = bf16[4,96,896]{2,1,0:T(8,128)(2,1)S(1)} all-gather(bf16[4,48,896]{2,1,0:T(8,128)(2,1)S(1)} %bitcast.133), channel_id=1, replica_groups=mesh['tm'=16,'chan'=2] {'chan'}, dimensions={1}, use_global_device_ids=true | all-gather | bytes 1032192 | tf_op jit(solution)/shard_map/all_gather | solution.py:112
  97.7 1.1 copy.31
  98.8 0.8 copy.32
  99.6 40.7 %psum.15 = f32[48]{0:T(128)} all-reduce(f32[48]{0:T(128)S(1)} %broadcast_multiply_fusion), channel_id=1, replica_groups=mesh['tm'=16,'chan'=2] {'tm'}, use_global_device_ids=true, to_apply=%region_4.5 | all-reduce | flops 48 | bytes 384 | tf_op jit(solution)/shard_map/psum | solution.py:122
  140.3 1.0 convert_element_type.41
  142.1 79.2 %all-reduce.4.cloned.1.call-done = f32[27,48,96]{2,1,0:T(8,128)} async-done(((f32[27,48,96]{2,1,0:T(8,128)}), f32[27,48,96]{2,1,0:T(8,128)}) %all-reduce.4.cloned.1.call-update) | async-done | bytes 497680 | tf_op jit(solution)/shard_map/psum | solution.py:122
  221.3 2.0 copy.65
  (54 shorter events, 7.7 us)
Async XLA Ops:
  7.2 9.5 %copy-start.5 = (bf16[48,2,896]{2,1,0:T(2,128)(2,1)S(1)}, bf16[48,2,896]{2,1,0:T(2,128)(2,1)}, u32[]{:S(2)}) copy-start(bf16[48,2,896]{2,1,0:T(2,128)(2,1)} %param.4) | copy-start | bytes 516100
  7.2 48.8 %reduce-scatter.3.cloned.1.call-start = ((), (), s32[]{:S(2)}) async-start(), calls=%async_computation.2 | async-start | bytes 1032192 | tf_op jit(solution)/shard_map/reduce_scatter | solution.py:91
  8.2 8.5 %collective-permute-start = (bf16[48,2,896]{2,0,1:T(8,128)(2,1)S(1)}, bf16[48,2,896]{2,0,1:T(8,128)(2,1)S(1)}, u32[]{:S(2)}, u32[]{:S(2)}) collective-permute-start(bf16[48,2,896]{2,0,1:T(8,128)(2,1)S(1)} %copy.21), channel_id=1, source_target_pairs={{0,2},{2,4},{4,6},{6,8},{8,10},{10,12},{12,14},{14,16},{16,18},{18... | collective-permute-start | bytes 516104 | tf_op jit(solution)/shard_map/ppermute | solution.py:15
  39.2 4.6 %copy-start.8 = (bf16[9,96,48]{1,2,0:T(8,128)(2,1)S(1)}, bf16[9,96,48]{1,2,0:T(8,128)(2,1)}, u32[]{:S(2)}) copy-start(bf16[9,96,48]{1,2,0:T(8,128)(2,1)} %copy.42) | copy-start | bytes 248836
  42.3 1.9 copy-start.9
  43.7 1.8 copy-start.10
  45.5 94.8 %reduce-scatter.5.cloned.1.call-start = ((), (), s32[]{:S(2)}) async-start(), calls=%async_computation.3 | async-start | bytes 1032192 | tf_op jit(solution)/shard_map/reduce_scatter | solution.py:108
  58.0 8.5 %copy-start = (bf16[48,2,896]{2,0,1:T(8,128)(2,1)}, bf16[48,2,896]{2,0,1:T(8,128)(2,1)S(1)}, u32[]{:S(2)}) copy-start(bf16[48,2,896]{2,0,1:T(8,128)(2,1)S(1)} %get-tuple-element.13) | copy-start | bytes 516100
  58.0 8.5 %collective-permute-start.1 = (bf16[48,2,896]{2,0,1:T(8,128)(2,1)S(1)}, bf16[48,2,896]{2,0,1:T(8,128)(2,1)S(1)}, u32[]{:S(2)}, u32[]{:S(2)}) collective-permute-start(bf16[48,2,896]{2,0,1:T(8,128)(2,1)S(1)} %get-tuple-element.13), channel_id=1, source_target_pairs={{2,0},{4,2},{6,4},{8,6},{10,8},{12,10},{14,12},{16,14},{18,16},{20... | collective-permute-start | bytes 516104 | tf_op jit(solution)/shard_map/ppermute | solution.py:15
  66.5 0.7 copy-start.7
  86.6 5.3 %copy-start.4 = (bf16[4,1,48,896]{3,2,0,1:T(8,128)(2,1)S(1)}, bf16[4,1,48,896]{3,2,0,1:T(8,128)(2,1)}, u32[]{:S(2)}) copy-start(bf16[4,1,48,896]{3,2,0,1:T(8,128)(2,1)} %stack_reshape.69) | copy-start | bytes 1032196
  86.6 5.3 %copy-start.2 = (bf16[4,1,48,896]{3,2,0,1:T(8,128)(2,1)S(1)}, bf16[4,1,48,896]{3,2,0,1:T(8,128)(2,1)}, u32[]{:S(2)}) copy-start(bf16[4,1,48,896]{3,2,0,1:T(8,128)(2,1)} %stack_reshape.70) | copy-start | bytes 1032196
  86.6 5.4 %copy-start.3 = (bf16[4,1,48,896]{3,2,0,1:T(8,128)(2,1)S(1)}, bf16[4,1,48,896]{3,2,0,1:T(8,128)(2,1)}, u32[]{:S(2)}) copy-start(bf16[4,1,48,896]{3,2,0,1:T(8,128)(2,1)} %stack_reshape.71) | copy-start | bytes 1032196
  86.6 5.4 %copy-start.1 = (bf16[27,96,96]{2,1,0:T(8,128)(2,1)S(1)}, bf16[27,96,96]{2,1,0:T(8,128)(2,1)}, u32[]{:S(2)}) copy-start(bf16[27,96,96]{2,1,0:T(8,128)(2,1)} %param.5) | copy-start | bytes 1492996
  94.1 127.1 %all-reduce.4.cloned.1.call-start = ((), (), s32[]{:S(2)}) async-start(), calls=%async_computation.4 | async-start | bytes 1327104 | tf_op jit(solution)/shard_map/psum | solution.py:122
  96.9 1.9 copy-start.6
Sparse Core Ops, SparseCore 0:
  45.6 10.3 reduce-scatter.2
  94.2 10.1 reduce-scatter.4
  110.4 110.8 all-reduce.3
where the time goes:
time: 231 us; the launch traced here: 230 us
  waiting for transfers between devices  97.3 us (42%)
  local copies, waits for them, and re-layouts  60 us (26%)
  blocking collectives  43 us (19%)
  between operations  14.1 us (6%)
  starting transfers between devices  6.27 us (3%)
  matrix products  4.85 us (2%)
  other arithmetic  4.22 us (2%)
    psum x1, waiting for transfers between devices, by_channels(): grad_weight, grad_bias = lax.psum((local_weight, local_bias), 'tm')  79.2 us
    psum x1, blocking collectives, by_channels(): grad_weight, grad_bias = lax.psum((local_weight, local_bias), 'tm')  40.7 us
    another operation x18, local copies, waits for them, and re-layouts, tap_stack(): return jnp.stack(layers, 1).reshape(frames, 9 * channels, pixels)  32.4 us
    unnamed x45, local copies, waits for them, and re-layouts  19.4 us
    reduce_scatter x1, waiting for transfers between devices, by_channels(): lax.psum_scatter(time_taps(kernels, inputs_stack, frames, False), 'chan',...  10.5 us
    ppermute x2, waiting for transfers between devices, shifted_2(): lax.ppermute(value, axis, [(source, source + steps) for source in range(f...  7.65 us
    ppermute x2, starting transfers between devices, shifted_2(): lax.ppermute(value, axis, [(source, source + steps) for source in range(f...  6.14 us
  transfers between devices with their start and end apart: 5, of which 4 were waited for; matrix products, arithmetic and copies ran while one was open for 3% of the time, Pallas kernels for 0%

commit v1 on v0

v1 whole, which is shorter than its diff:
```python
import functools
import math

import jax
import jax.numpy as jnp
from jax import lax
from jax.experimental import pallas as pl
from jax.experimental.pallas import tpu as pltpu
from jax.sharding import PartitionSpec as P

HGT = 8
WID = 112
MESH = pl.DeviceIdType.MESH
F32 = jnp.float32
BF16 = jnp.bfloat16


def dot(a, b):
    return jnp.dot(a, b, preferred_element_type=F32)


def dot_nt(a, b):
    return lax.dot_general(a, b, (((1,), (1,)), ((), ())), preferred_element_type=F32)


def border_masks(pix):
    place = lax.broadcasted_iota(jnp.int32, (1, pix), 1)
    row = jnp.zeros((1, pix), jnp.int32)
    for k in range(1, HGT):
        row = row + (place >= k * WID).astype(jnp.int32)
    col = place - row * WID
    return (
        (row >= 1).astype(F32),
        (row <= HGT - 2).astype(F32),
        (col >= 1).astype(F32),
        (col <= WID - 2).astype(F32),
    )


def kernel(
    n, scale, norm,
    x_ref, w_ref, b_ref, cot_ref,
    out_ref, gin_ref, gw_ref, gb_ref,
    xe, ge, w_early, w_own, v_own, v_late, y, g9, pack, parts, whole,
    x_send, x_recv, g_send, g_recv, rs_send, rs_recv, ag_send, ag_recv,
):
    own = x_ref.shape[1]
    pix = x_ref.shape[2]
    full = 2 * own
    chunk = pack.shape[0] // n
    me = lax.axis_index("tm")
    ch = lax.axis_index("chan")
    other = 1 - ch
    half = pl.multiple_of(ch * own, 16)
    nxt = lax.rem(me + 1, n)
    prv = lax.rem(me + n - 1, n)

    barrier = pltpu.get_barrier_semaphore()

    def greet(d, carry):
        pl.semaphore_signal(
            barrier, inc=1, device_id=(lax.rem(me + d, n), ch), device_id_type=MESH
        )
        return carry

    pl.semaphore_signal(barrier, inc=1, device_id=(me, other), device_id_type=MESH)
    lax.fori_loop(1, n, greet, 0)

    def rows(frame):
        return pl.ds(pl.multiple_of(frame * full + ch * own, 16), own)

    def copy(buf, src, dst, sems, k, device):
        return pltpu.make_async_remote_copy(
            src_ref=buf.at[rows(src)],
            dst_ref=buf.at[rows(dst)],
            send_sem=sems[0].at[k],
            recv_sem=sems[1].at[k],
            device_id=device,
            device_id_type=MESH,
        )

    xs, gs = (x_send, x_recv), (g_send, g_recv)
    for f in range(2):
        xe[rows(2 + f), :] = x_ref[f]
    pl.semaphore_wait(barrier, n)

    def x_share(f):
        return copy(xe, 2 + f, 2 + f, xs, f, (me, other))

    def x_halo(f):
        return copy(xe, 2 + f, f, xs, 2 + f, (nxt, ch))

    def x_relay(f):
        return copy(xe, f, f, xs, 4 + f, (me, other))

    def g_share(f):
        return copy(ge, f, f, gs, f, (me, other))

    def g_halo(f):
        return copy(ge, f, 2 + f, gs, 2 + f, (prv, ch))

    def g_relay(f):
        return copy(ge, 2 + f, 2 + f, gs, 4 + f, (me, other))

    first, last = me == 0, me == n - 1

    @pl.when(jnp.logical_not(last))
    def _():
        x_halo(1).start()
        x_halo(0).start()

    x_share(0).start()
    x_share(1).start()

    @pl.when(first)
    def _():
        xe[0 : 2 * full, :] = jnp.zeros((2 * full, pix), BF16)

    @pl.when(last)
    def _():
        ge[2 * full : 4 * full, :] = jnp.zeros((2 * full, pix), BF16)

    for tap in range(9):
        to = pl.ds(tap * own, own)
        w0, w1, w2 = (w_ref[9 * t + tap, pl.ds(half, own), :] for t in range(3))
        w_early[to, 0:full] = w0
        w_early[to, full : 2 * full] = w1
        w_own[to, 0:full] = w1
        w_own[to, full : 2 * full] = w2
        v0, v1, v2 = (w_ref[9 * t + tap].T for t in range(3))
        v_own[tap, :, 0:full] = v2
        v_own[tap, :, full : 2 * full] = v1
        v_late[tap, :, 0:full] = v1
        v_late[tap, :, full : 2 * full] = v0

    above, below, left, right = border_masks(pix)

    def spatial_sum(f, block, height, sign):
        def at(kh, kw):
            if sign < 0:
                kh, kw = 2 - kh, 2 - kw
            return y[f, pl.ds((3 * kh + kw) * own + block, height), :]

        z = []
        for kw in range(3):
            z.append(
                at(1, kw)
                + above * pltpu.roll(at(0, kw), WID, 1)
                + below * pltpu.roll(at(2, kw), pix - WID, 1)
            )
        return z[1] + left * pltpu.roll(z[0], 1, 1) + right * pltpu.roll(z[2], pix - 1, 1)

    x_share(0).wait_recv()
    x_share(1).wait_recv()
    taps = 9 * own
    w_last = jnp.concatenate([w_ref[18 + t, pl.ds(half, own), :] for t in range(9)], 0)
    y[0] = dot(w_last, xe[2 * full : 3 * full, :])
    y[1] = dot(w_own[...], xe[2 * full : 4 * full, :])

    @pl.when(jnp.logical_not(first))
    def _():
        for f in (1, 0):
            x_halo(f).wait_recv()
            x_relay(f).start()
        for f in (1, 0):
            x_relay(f).wait_recv()

    bias_sums = []
    for f in (1, 0):
        if f == 1:
            y[1] += dot(w_early[:, 0:full], xe[full : 2 * full, :])
        else:
            y[0] += dot(w_early[...], xe[0 : 2 * full, :])
        sums = []
        for block in range(0, own, 16):
            pre = spatial_sum(f, block, 16, 1) + b_ref[block : block + 16, :].astype(F32)
            sig = jax.nn.sigmoid(pre)
            out_ref[f, block : block + 16, :] = (pre * sig).astype(BF16)
            cot = cot_ref[f, block : block + 16, :].astype(F32)
            grad = (cot * sig * (1.0 + pre * (1.0 - sig))).astype(BF16)
            ge[pl.ds(pl.multiple_of(f * full + ch * own + block, 16), 16), :] = grad
            grad = grad.astype(F32)
            sums.append(jnp.sum(grad, axis=1, keepdims=True))
            moved = (
                right * pltpu.roll(grad, pix - 1, 1),
                grad,
                left * pltpu.roll(grad, 1, 1),
            )
            for kw in range(3):
                shifted = (
                    below * pltpu.roll(moved[kw], pix - WID, 1),
                    moved[kw],
                    above * pltpu.roll(moved[kw], WID, 1),
                )
                for kh in range(3):
                    g9[f, pl.ds((3 * kh + kw) * own + block, 16), :] = shifted[kh].astype(BF16)
        bias_sums.append(jnp.concatenate(sums, 0))
        g_share(f).start()

        @pl.when(jnp.logical_not(first))
        def _():
            g_halo(f).start()

    rest = 3 * full - 256
    piece = 112
    base = 2 * taps
    product = dot_nt(g9[0], xe[0 : 3 * full, :]) + dot_nt(g9[1], xe[full : 4 * full, :])
    pack[0:taps, :] = product[:, 0:128].astype(BF16)
    pack[taps:base, :] = product[:, 128:256].astype(BF16)
    if pack.shape[0] > base:
        pack[base:, :] = jnp.zeros((pack.shape[0] - base, 128), BF16)
    for k in range(4):
        stop = min(taps, (k + 1) * piece)
        pack[base : base + stop - k * piece, rest * k : rest * (k + 1)] = product[
            k * piece : stop, 256 : 256 + rest
        ].astype(BF16)
    lane = lax.broadcasted_iota(jnp.int32, (own, 128), 1)
    pack[base + piece : base + piece + own, :] = jnp.where(
        lane == 0, jnp.broadcast_to(bias_sums[0] + bias_sums[1], (own, 128)), 0.0
    ).astype(BF16)

    def part(i):
        return pl.ds(pl.multiple_of(i * chunk, 16), chunk)

    def rs_copy(d):
        to = lax.rem(me + d, n)
        return pltpu.make_async_remote_copy(
            src_ref=pack.at[part(to)],
            dst_ref=parts.at[d],
            send_sem=rs_send.at[d],
            recv_sem=rs_recv.at[d],
            device_id=(to, ch),
            device_id_type=MESH,
        )

    def ag_copy(d):
        return pltpu.make_async_remote_copy(
            src_ref=whole.at[part(me)],
            dst_ref=whole.at[part(me)],
            send_sem=ag_send.at[d],
            recv_sem=ag_recv.at[d],
            device_id=(lax.rem(me + d, n), ch),
            device_id_type=MESH,
        )

    def ag_arrival(d):
        come = part(lax.rem(me + n - d, n))
        return pltpu.make_async_remote_copy(
            src_ref=whole.at[come],
            dst_ref=whole.at[come],
            send_sem=ag_send.at[d],
            recv_sem=ag_recv.at[d],
            device_id=(lax.rem(me + d, n), ch),
            device_id_type=MESH,
        )

    def each(act):
        def step(d, carry):
            act(d)
            return carry

        lax.fori_loop(1, n, step, 0)

    each(lambda d: rs_copy(d).start())

    @pl.when(jnp.logical_not(last))
    def _():
        for f in (1, 0):
            g_halo(f).wait_recv()
            g_relay(f).start()

    g_share(1).wait_recv()
    g_share(0).wait_recv()
    v_mine = v_own[:, pl.ds(half, own), :].reshape(taps, 2 * full)
    y[0] = dot(v_mine, ge[0 : 2 * full, :])
    y[1] = dot(v_mine[:, 0:full], ge[full : 2 * full, :])

    def add_part(d, total):
        rs_copy(d).wait_recv()
        return total + parts[d].astype(F32)

    total = lax.fori_loop(1, n, add_part, pack[part(me), :].astype(F32))
    whole[part(me), :] = total.astype(BF16)
    each(lambda d: ag_copy(d).start())

    @pl.when(jnp.logical_not(last))
    def _():
        for f in (1, 0):
            g_relay(f).wait_recv()

    v_other = v_late[:, pl.ds(half, own), :].reshape(taps, 2 * full)
    v_first = jnp.concatenate(
        [v_late[t, pl.ds(half, own), full : 2 * full] for t in range(9)], 0
    )
    y[0] += dot(v_first, ge[2 * full : 3 * full, :])
    y[1] += dot(v_other, ge[2 * full : 4 * full, :])
    for f in range(2):
        for block in range(0, own, 16):
            gin_ref[f, block : block + 16, :] = spatial_sum(f, block, 16, -1).astype(BF16)

    each(lambda d: ag_arrival(d).wait_recv())
    top = whole[0:taps, :].astype(F32) * norm
    mid = whole[taps:base, :].astype(F32) * norm
    tail = jnp.concatenate(
        [
            whole[base : base + min(taps, (k + 1) * piece) - k * piece, :].astype(F32)[
                :, rest * k : rest * (k + 1)
            ]
            for k in range(4)
        ],
        0,
    ) * norm
    gw_ref[0:9, :, :] = top[:, 0:full].reshape(9, own, full)
    gw_ref[9:18, :, 0 : 128 - full] = top[:, full:128].reshape(9, own, 128 - full)
    gw_ref[9:18, :, 128 - full : full] = mid[:, 0 : 2 * full - 128].reshape(9, own, 2 * full - 128)
    gw_ref[18:27, :, 0 : 256 - 2 * full] = mid[:, 2 * full - 128 : 128].reshape(
        9, own, 256 - 2 * full
    )
    gw_ref[18:27, :, 256 - 2 * full : full] = tail.reshape(9, own, rest)
    ones = jnp.ones((8, 128), BF16)
    gb_ref[...] = dot_nt(ones, whole[base + piece : base + piece + own, :])[0:1, :] * norm

    for f in range(2):
        x_share(f).wait_send()
        g_share(f).wait_send()

    @pl.when(jnp.logical_not(last))
    def _():
        for f in range(2):
            x_halo(f).wait_send()
            g_relay(f).wait_send()

    @pl.when(jnp.logical_not(first))
    def _():
        for f in range(2):
            g_halo(f).wait_send()
            x_relay(f).wait_send()

    each(lambda d: rs_copy(d).wait_send())
    each(lambda d: ag_copy(d).wait_send())


def local(latents, weight, conv_bias, cotangent):
    own, frames, pix = latents.shape
    n = lax.axis_size("tm")
    full = weight.shape[1]
    norm = 1.0 / math.sqrt(frames * n * pix)
    need = 2 * 9 * own + 112 + own
    chunk = -(-need // (16 * n)) * 16
    vmem = pl.BlockSpec(memory_space=pltpu.VMEM)
    dma = pltpu.SemaphoreType.DMA
    out, gin, gw, gb = pl.pallas_call(
        functools.partial(kernel, n, None, norm),
        out_shape=(
            jax.ShapeDtypeStruct((frames, own, pix), BF16),
            jax.ShapeDtypeStruct((frames, own, pix), BF16),
            jax.ShapeDtypeStruct((27, own, full), F32),
            jax.ShapeDtypeStruct((1, own), F32),
        ),
        in_specs=[vmem] * 4,
        out_specs=(vmem,) * 4,
        scratch_shapes=[
            pltpu.VMEM((4 * full, pix), BF16),
            pltpu.VMEM((4 * full, pix), BF16),
            pltpu.VMEM((9 * own, 2 * full), BF16),
            pltpu.VMEM((9 * own, 2 * full), BF16),
            pltpu.VMEM((9, full, 2 * full), BF16),
            pltpu.VMEM((9, full, 2 * full), BF16),
            pltpu.VMEM((2, 9 * own, pix), F32),
            pltpu.VMEM((2, 9 * own, pix), BF16),
            pltpu.VMEM((n * chunk, 128), BF16),
            pltpu.VMEM((n, chunk, 128), BF16),
            pltpu.VMEM((n * chunk, 128), BF16),
            dma((6,)), dma((6,)), dma((6,)), dma((6,)),
            dma((n,)), dma((n,)), dma((n,)), dma((n,)),
        ],
        compiler_params=pltpu.CompilerParams(
            collective_id=0, has_side_effects=True, vmem_limit_bytes=48 * 1024 * 1024
        ),
    )(
        latents.transpose(1, 0, 2),
        weight,
        conv_bias.reshape(own, 1),
        cotangent.transpose(1, 0, 2),
    )
    return out.transpose(1, 0, 2), gin.transpose(1, 0, 2), gw, gb.reshape(own)


def solution(mesh):
    in_specs = (P("chan", "tm", None), P(), P("chan"), P("chan", "tm", None))
    out_specs = (P("chan", "tm", None), P("chan", "tm", None), P(None, "chan", None), P("chan"))
    return jax.shard_map(local, mesh=mesh, in_specs=in_specs, out_specs=out_specs, check_vma=False)
```

time: 231 us -> 37.2 us (0.16)
  waiting for transfers between devices: 97.3 us -> 0 us
  local copies, waits for them, and re-layouts: 60 us -> 4.74 us
  blocking collectives: 43 us -> 0 us
  Pallas kernels: 0 us -> 31.7 us
  between operations: 14.1 us -> 0.67 us
  starting transfers between devices: 6.27 us -> 0 us
  matrix products: 4.85 us -> 0 us
  other arithmetic: 4.22 us -> 0 us
    psum x1 -> x0, waiting for transfers between devices: 79.2 us -> none  [by_channels(): grad_weight, grad_bias = lax.psum((local_weight, local_bias), 'tm')]
    psum x1 -> x0, blocking collectives: 40.7 us -> none  [by_channels(): grad_weight, grad_bias = lax.psum((local_weight, local_bias), 'tm')]
    another operation x18 -> x0, local copies, waits for them, and re-layouts: 32.4 us -> none  [tap_stack(): return jnp.stack(layers, 1).reshape(frames, 9 * channels, pixels)]
    pallas_call x0 -> x1, Pallas kernels: none -> 31.7 us  [local(): pl.pallas_call(functools.partial(kernel, n, None, norm), out_shape=(jax.S...]
    unnamed x45 -> x8, local copies, waits for them, and re-layouts: 19.4 us -> 3.6 us
    reduce_scatter x2 -> x0, waiting for transfers between devices: 10.5 us -> none  [the longest x1 10.5 us: by_channels(): lax.psum_scatter(time_taps(kernels, inputs_stack, frames, False), 'chan',...]
    ppermute x2 -> x0, waiting for transfers between devices: 7.65 us -> none  [shifted_2(): lax.ppermute(value, axis, [(source, source + steps) for source in range(f...]
    ppermute x2 -> x0, starting transfers between devices: 6.14 us -> none  [shifted_2(): lax.ppermute(value, axis, [(source, source + steps) for source in range(f...]
  transfers between devices with their start and end apart: 5 -> 0, of which waited for: 4 -> 0; matrix products, arithmetic and copies ran while one was open for 3% -> 0% of each run, Pallas kernels for 0% -> 0%
where the time goes in v1:
time: 37.2 us; the launch traced here: 37.1 us
  Pallas kernels  31.7 us (85%)
  local copies, waits for them, and re-layouts  4.74 us (13%)
  between operations  0.67 us (2%)
    pallas_call x1, Pallas kernels, local(): pl.pallas_call(functools.partial(kernel, n, None, norm), out_shape=(jax.S...  31.7 us
    unnamed x8, local copies, waits for them, and re-layouts  3.6 us
    transpose x1, local copies, waits for them, and re-layouts, local(): cotangent.transpose(1, 0, 2)  1.04 us

profile of v1, /device:TPU:0, one launch (start us, length us, event | category | flops | bytes accessed | tf_op | source)
XLA Modules:
  0.0 37.1 jit_solution(16880735226235280422)
XLA Ops:
  0.6 0.0 copy-start.1
  0.6 0.0 copy-start
  0.7 0.6 %copy-done.1 = bf16[48]{0:T(256)(128)(2,1)S(1)} copy-done((bf16[48]{0:T(256)(128)(2,1)S(1)}, bf16[48]{0:T(256)(128)(2,1)}, u32[]{:S(2)}) %copy-start.1) | copy-done | bytes 120
  1.3 0.1 copy.10.b_ref
  1.4 1.0 %copy_bitcast_fusion = (bf16[2,48,896]{2,1,0:T(8,128)(2,1)S(1)}, bf16[2,48,896]{2,1,0:T(8,128)(2,1)S(1)}) fusion(bf16[48,2,896]{2,1,0:T(2,128)(2,1)} %param.7, bf16[48,2,896]{2,1,0:T(2,128)(2,1)} %param.4), kind=kLoop, calls=%fused_computation | loop fusion | bytes 688128 | tf_op jit(solution)/shard_map/transpose | solution.py:384
  2.4 0.0 copy-done
  2.4 31.7 %shard_map.75 = (bf16[2,48,896]{2,1,0:T(8,128)(2,1)S(1)}, bf16[2,48,896]{2,1,0:T(8,128)(2,1)S(1)}, f32[27,48,96]{2,1,0:T(8,128)S(1)}, f32[1,48]{1,0:T(1,128)S(1)}) custom-call(bf16[2,48,896]{2,1,0:T(8,128)(2,1)S(1)} %get-tuple-element.17.x_ref, bf16[27,96,96]{2,1,0:T(8,128)(2,1)S(1)} %copy-done, bf16[48,1]{1,0:T(8,128)(2,1)S(1)} %copy.10.b_ref, ...), custom_call_target="tpu_custom_call" | custom-call | tf_op jit(solution)/shard_map/pallas_call | solution.py:352
  34.1 0.8 %copy.11 = bf16[48,2,896]{2,1,0:T(2,128)(2,1)} copy(bf16[48,2,896]{2,0,1:T(8,128)(2,1)S(1)} %bitcast.9) | data formatting | bytes 344064
  34.9 0.8 %copy.12 = bf16[48,2,896]{2,1,0:T(2,128)(2,1)} copy(bf16[48,2,896]{2,0,1:T(8,128)(2,1)S(1)} %bitcast.8) | data formatting | bytes 344064
  35.7 0.8 %copy.17 = f32[27,48,96]{2,1,0:T(8,128)} copy(f32[27,48,96]{2,1,0:T(8,128)S(1)} %get-tuple-element.24) | data formatting | bytes 995328
  36.6 0.5 %copy.18 = f32[48]{0:T(128)} copy(f32[48]{0:T(128)S(1)} %bitcast.10) | data formatting | bytes 384
Async XLA Ops:
  0.6 0.7 %copy-start.1 = (bf16[48]{0:T(256)(128)(2,1)S(1)}, bf16[48]{0:T(256)(128)(2,1)}, u32[]{:S(2)}) copy-start(bf16[48]{0:T(256)(128)(2,1)} %param.6) | copy-start | bytes 292
  0.6 1.8 %copy-start = (bf16[27,96,96]{2,1,0:T(8,128)(2,1)S(1)}, bf16[27,96,96]{2,1,0:T(8,128)(2,1)}, u32[]{:S(2)}) copy-start(bf16[27,96,96]{2,1,0:T(8,128)(2,1)} %w_ref.1) | copy-start | bytes 1492996

commit v2 on v1

--- a/solution.py
+++ b/solution.py
@@ -38,10 +38,10 @@
 
 
 def kernel(
-    n, scale, norm,
+    n,
     x_ref, w_ref, b_ref, cot_ref,
-    out_ref, gin_ref, gw_ref, gb_ref,
-    xe, ge, w_early, w_own, v_own, v_late, y, g9, pack, parts, whole,
+    out_ref, gin_ref, whole,
+    xe, ge, w_early, w_own, v_own, v_late, y, g9, pack, parts,
     x_send, x_recv, g_send, g_recv, rs_send, rs_recv, ag_send, ag_recv,
 ):
     own = x_ref.shape[1]
@@ -82,43 +82,6 @@
     xs, gs = (x_send, x_recv), (g_send, g_recv)
     for f in range(2):
         xe[rows(2 + f), :] = x_ref[f]
-    pl.semaphore_wait(barrier, n)
-
-    def x_share(f):
-        return copy(xe, 2 + f, 2 + f, xs, f, (me, other))
-
-    def x_halo(f):
-        return copy(xe, 2 + f, f, xs, 2 + f, (nxt, ch))
-
-    def x_relay(f):
-        return copy(xe, f, f, xs, 4 + f, (me, other))
-
-    def g_share(f):
-        return copy(ge, f, f, gs, f, (me, other))
-
-    def g_halo(f):
-        return copy(ge, f, 2 + f, gs, 2 + f, (prv, ch))
-
-    def g_relay(f):
-        return copy(ge, 2 + f, 2 + f, gs, 4 + f, (me, other))
-
-    first, last = me == 0, me == n - 1
-
-    @pl.when(jnp.logical_not(last))
-    def _():
-        x_halo(1).start()
-        x_halo(0).start()
-
-    x_share(0).start()
-    x_share(1).start()
-
-    @pl.when(first)
-    def _():
-        xe[0 : 2 * full, :] = jnp.zeros((2 * full, pix), BF16)
-
-    @pl.when(last)
-    def _():
-        ge[2 * full : 4 * full, :] = jnp.zeros((2 * full, pix), BF16)
 
     for tap in range(9):
         to = pl.ds(tap * own, own)
@@ -133,6 +96,44 @@
         v_late[tap, :, 0:full] = v1
         v_late[tap, :, full : 2 * full] = v0
 
+    pl.semaphore_wait(barrier, n)
+
+    def x_share(f):
+        return copy(xe, 2 + f, 2 + f, xs, f, (me, other))
+
+    def x_halo(f):
+        return copy(xe, 2 + f, f, xs, 2 + f, (nxt, ch))
+
+    def x_relay(f):
+        return copy(xe, f, f, xs, 4 + f, (me, other))
+
+    def g_share(f):
+        return copy(ge, f, f, gs, f, (me, other))
+
+    def g_halo(f):
+        return copy(ge, f, 2 + f, gs, 2 + f, (prv, ch))
+
+    def g_relay(f):
+        return copy(ge, 2 + f, 2 + f, gs, 4 + f, (me, other))
+
+    first, last = me == 0, me == n - 1
+
+    @pl.when(jnp.logical_not(last))
+    def _():
+        x_halo(1).start()
+        x_halo(0).start()
+
+    x_share(0).start()
+    x_share(1).start()
+
+    @pl.when(first)
+    def _():
+        xe[0 : 2 * full, :] = jnp.zeros((2 * full, pix), BF16)
+
+    @pl.when(last)
+    def _():
+        ge[2 * full : 4 * full, :] = jnp.zeros((2 * full, pix), BF16)
+
     above, below, left, right = border_masks(pix)
 
     def spatial_sum(f, block, height, sign):
@@ -150,6 +151,12 @@
             )
         return z[1] + left * pltpu.roll(z[0], 1, 1) + right * pltpu.roll(z[2], pix - 1, 1)
 
+    eye = lax.broadcasted_iota(jnp.int32, (own, own), 0) == lax.broadcasted_iota(
+        jnp.int32, (own, own), 1
+    )
+    spread = jnp.where(eye, jnp.broadcast_to(b_ref[...].astype(F32), (own, own)), 0.0)
+    bias = dot(spread.astype(BF16), jnp.ones((own, 128), BF16))
+
     x_share(0).wait_recv()
     x_share(1).wait_recv()
     taps = 9 * own
@@ -157,23 +164,23 @@
     y[0] = dot(w_last, xe[2 * full : 3 * full, :])
     y[1] = dot(w_own[...], xe[2 * full : 4 * full, :])
 
-    @pl.when(jnp.logical_not(first))
-    def _():
-        for f in (1, 0):
+    def x_forward(f):
+        @pl.when(jnp.logical_not(first))
+        def _():
             x_halo(f).wait_recv()
             x_relay(f).start()
-        for f in (1, 0):
+
+    def x_arrived(f):
+        @pl.when(jnp.logical_not(first))
+        def _():
             x_relay(f).wait_recv()
 
-    bias_sums = []
-    for f in (1, 0):
-        if f == 1:
-            y[1] += dot(w_early[:, 0:full], xe[full : 2 * full, :])
-        else:
-            y[0] += dot(w_early[...], xe[0 : 2 * full, :])
+    def activate(f, between):
         sums = []
         for block in range(0, own, 16):
-            pre = spatial_sum(f, block, 16, 1) + b_ref[block : block + 16, :].astype(F32)
+            if block == own - 16:
+                between()
+            pre = spatial_sum(f, block, 16, 1) + bias[block : block + 16, 0:1]
             sig = jax.nn.sigmoid(pre)
             out_ref[f, block : block + 16, :] = (pre * sig).astype(BF16)
             cot = cot_ref[f, block : block + 16, :].astype(F32)
@@ -194,17 +201,27 @@
                 )
                 for kh in range(3):
                     g9[f, pl.ds((3 * kh + kw) * own + block, 16), :] = shifted[kh].astype(BF16)
-        bias_sums.append(jnp.concatenate(sums, 0))
         g_share(f).start()
 
         @pl.when(jnp.logical_not(first))
         def _():
             g_halo(f).start()
 
+        return jnp.concatenate(sums, 0)
+
+    x_forward(1)
+    x_arrived(1)
+    y[1] += dot(w_early[:, 0:full], xe[full : 2 * full, :])
+    bias_sum = activate(1, lambda: x_forward(0))
+    product = dot_nt(g9[1], xe[full : 4 * full, :])
+    x_arrived(0)
+    y[0] += dot(w_early[...], xe[0 : 2 * full, :])
+    bias_sum += activate(0, lambda: None)
+
     rest = 3 * full - 256
     piece = 112
     base = 2 * taps
-    product = dot_nt(g9[0], xe[0 : 3 * full, :]) + dot_nt(g9[1], xe[full : 4 * full, :])
+    product += dot_nt(g9[0], xe[0 : 3 * full, :])
     pack[0:taps, :] = product[:, 0:128].astype(BF16)
     pack[taps:base, :] = product[:, 128:256].astype(BF16)
     if pack.shape[0] > base:
@@ -216,7 +233,7 @@
         ].astype(BF16)
     lane = lax.broadcasted_iota(jnp.int32, (own, 128), 1)
     pack[base + piece : base + piece + own, :] = jnp.where(
-        lane == 0, jnp.broadcast_to(bias_sums[0] + bias_sums[1], (own, 128)), 0.0
+        lane == 0, jnp.broadcast_to(bias_sum, (own, 128)), 0.0
     ).astype(BF16)
 
     def part(i):
@@ -263,17 +280,17 @@
 
     each(lambda d: rs_copy(d).start())
 
-    @pl.when(jnp.logical_not(last))
-    def _():
-        for f in (1, 0):
-            g_halo(f).wait_recv()
-            g_relay(f).start()
-
     g_share(1).wait_recv()
     g_share(0).wait_recv()
     v_mine = v_own[:, pl.ds(half, own), :].reshape(taps, 2 * full)
     y[0] = dot(v_mine, ge[0 : 2 * full, :])
     y[1] = dot(v_mine[:, 0:full], ge[full : 2 * full, :])
+
+    @pl.when(jnp.logical_not(last))
+    def _():
+        for f in (1, 0):
+            g_halo(f).wait_recv()
+            g_relay(f).start()
 
     def add_part(d, total):
         rs_copy(d).wait_recv()
@@ -299,6 +316,31 @@
             gin_ref[f, block : block + 16, :] = spatial_sum(f, block, 16, -1).astype(BF16)
 
     each(lambda d: ag_arrival(d).wait_recv())
+    for f in range(2):
+        x_share(f).wait_send()
+        g_share(f).wait_send()
+
+    @pl.when(jnp.logical_not(last))
+    def _():
+        for f in range(2):
+            x_halo(f).wait_send()
+            g_relay(f).wait_send()
+
+    @pl.when(jnp.logical_not(first))
+    def _():
+        for f in range(2):
+            g_halo(f).wait_send()
+            x_relay(f).wait_send()
+
+    each(lambda d: rs_copy(d).wait_send())
+    each(lambda d: ag_copy(d).wait_send())
+
+
+def unpack(norm, own, full, whole, gw_ref, gb_ref):
+    taps = 9 * own
+    rest = 3 * full - 256
+    piece = 112
+    base = 2 * taps
     top = whole[0:taps, :].astype(F32) * norm
     mid = whole[taps:base, :].astype(F32) * norm
     tail = jnp.concatenate(
@@ -320,25 +362,6 @@
     ones = jnp.ones((8, 128), BF16)
     gb_ref[...] = dot_nt(ones, whole[base + piece : base + piece + own, :])[0:1, :] * norm
 
-    for f in range(2):
-        x_share(f).wait_send()
-        g_share(f).wait_send()
-
-    @pl.when(jnp.logical_not(last))
-    def _():
-        for f in range(2):
-            x_halo(f).wait_send()
-            g_relay(f).wait_send()
-
-    @pl.when(jnp.logical_not(first))
-    def _():
-        for f in range(2):
-            g_halo(f).wait_send()
-            x_relay(f).wait_send()
-
-    each(lambda d: rs_copy(d).wait_send())
-    each(lambda d: ag_copy(d).wait_send())
-
 
 def local(latents, weight, conv_bias, cotangent):
     own, frames, pix = latents.shape
@@ -349,16 +372,15 @@
     chunk = -(-need // (16 * n)) * 16
     vmem = pl.BlockSpec(memory_space=pltpu.VMEM)
     dma = pltpu.SemaphoreType.DMA
-    out, gin, gw, gb = pl.pallas_call(
-        functools.partial(kernel, n, None, norm),
+    out, gin, packed = pl.pallas_call(
+        functools.partial(kernel, n),
         out_shape=(
             jax.ShapeDtypeStruct((frames, own, pix), BF16),
             jax.ShapeDtypeStruct((frames, own, pix), BF16),
-            jax.ShapeDtypeStruct((27, own, full), F32),
-            jax.ShapeDtypeStruct((1, own), F32),
+            jax.ShapeDtypeStruct((n * chunk, 128), BF16),
         ),
         in_specs=[vmem] * 4,
-        out_specs=(vmem,) * 4,
+        out_specs=(vmem,) * 3,
         scratch_shapes=[
             pltpu.VMEM((4 * full, pix), BF16),
             pltpu.VMEM((4 * full, pix), BF16),
@@ -370,7 +392,6 @@
             pltpu.VMEM((2, 9 * own, pix), BF16),
             pltpu.VMEM((n * chunk, 128), BF16),
             pltpu.VMEM((n, chunk, 128), BF16),
-            pltpu.VMEM((n * chunk, 128), BF16),
             dma((6,)), dma((6,)), dma((6,)), dma((6,)),
             dma((n,)), dma((n,)), dma((n,)), dma((n,)),
         ],
@@ -380,9 +401,19 @@
     )(
         latents.transpose(1, 0, 2),
         weight,
-        conv_bias.reshape(own, 1),
+        conv_bias.reshape(1, own),
         cotangent.transpose(1, 0, 2),
     )
+    gw, gb = pl.pallas_call(
+        functools.partial(unpack, norm, own, full),
+        out_shape=(
+            jax.ShapeDtypeStruct((27, own, full), F32),
+            jax.ShapeDtypeStruct((1, own), F32),
+        ),
+        in_specs=[vmem],
+        out_specs=(vmem,) * 2,
+        compiler_params=pltpu.CompilerParams(vmem_limit_bytes=32 * 1024 * 1024),
+    )(packed)
     return out.transpose(1, 0, 2), gin.transpose(1, 0, 2), gw, gb.reshape(own)
 
 

time: 37.2 us -> 36.9 us (level)
  local copies, waits for them, and re-layouts: 4.74 us -> 3.39 us
  Pallas kernels: 31.7 us -> 32.7 us
    unnamed x8 -> x6, local copies, waits for them, and re-layouts: 3.6 us -> 2.29 us
    pallas_call x1 -> x2, Pallas kernels: 31.7 us -> 32.7 us  [the longest x1 31.5 us: local(): pl.pallas_call(functools.partial(kernel, n), out_shape=(jax.ShapeDtypeStr...]
where the time goes in v2:
time: 36.9 us; the launch traced here: 36.8 us
  Pallas kernels  32.7 us (89%)
  local copies, waits for them, and re-layouts  3.39 us (9%)
  between operations  0.66 us (2%)
    pallas_call x1, Pallas kernels, local(): pl.pallas_call(functools.partial(kernel, n), out_shape=(jax.ShapeDtypeStr...  31.5 us
    unnamed x6, local copies, waits for them, and re-layouts  2.29 us
    pallas_call x1, Pallas kernels, local(): pl.pallas_call(functools.partial(unpack, norm, own, full), out_shape=(jax...  1.16 us
    transpose x1, local copies, waits for them, and re-layouts, local(): cotangent.transpose(1, 0, 2)  1.1 us

profile of v2, /device:TPU:0, one launch (start us, length us, event | category | flops | bytes accessed | tf_op | source)
XLA Modules:
  0.0 36.8 jit_solution(1163049006607630372)
XLA Ops:
  0.6 0.0 copy-start
  0.6 1.1 %copy_bitcast_fusion = (bf16[2,48,896]{2,1,0:T(8,128)(2,1)S(1)}, bf16[2,48,896]{2,1,0:T(8,128)(2,1)S(1)}) fusion(bf16[48,2,896]{2,1,0:T(2,128)(2,1)} %param.7, bf16[48,2,896]{2,1,0:T(2,128)(2,1)} %param.4), kind=kLoop, calls=%fused_computation | loop fusion | bytes 688128 | tf_op jit(solution)/shard_map/transpose | solution.py:405
  1.7 0.0 copy-start.1
  1.8 0.1 copy-done
  1.9 0.6 %copy-done.1 = bf16[48]{0:T(256)(128)(2,1)S(1)} copy-done((bf16[48]{0:T(256)(128)(2,1)S(1)}, bf16[48]{0:T(256)(128)(2,1)}, u32[]{:S(2)}) %copy-start.1) | copy-done | bytes 120
  2.4 31.5 %shard_map.75 = (bf16[2,48,896]{2,1,0:T(8,128)(2,1)S(1)}, bf16[2,48,896]{2,1,0:T(8,128)(2,1)S(1)}, bf16[1024,128]{1,0:T(8,128)(2,1)S(1)}) custom-call(bf16[2,48,896]{2,1,0:T(8,128)(2,1)S(1)} %get-tuple-element.19.x_ref, bf16[27,96,96]{2,1,0:T(8,128)(2,1)S(1)} %copy-done, bf16[1,48]{1,0:T(2,128)(2,1)S(1)} %bitcast.10, ...), custom_call_target="tpu_custom_call" | custom-call | tf_op jit(solution)/shard_map/pallas_call | solution.py:375
  34.0 0.8 %copy.10 = bf16[48,2,896]{2,1,0:T(2,128)(2,1)} copy(bf16[48,2,896]{2,0,1:T(8,128)(2,1)S(1)} %bitcast.9) | data formatting | bytes 344064
  34.8 0.8 %copy.11 = bf16[48,2,896]{2,1,0:T(2,128)(2,1)} copy(bf16[48,2,896]{2,0,1:T(8,128)(2,1)S(1)} %bitcast.8) | data formatting | bytes 344064
  35.6 1.2 %shard_map.76 = (f32[27,48,96]{2,1,0:T(8,128)}, f32[1,48]{1,0:T(1,128)}) custom-call(bf16[1024,128]{1,0:T(8,128)(2,1)S(1)} %get-tuple-element.11.whole), custom_call_target="tpu_custom_call" | custom-call | tf_op jit(solution)/shard_map/pallas_call | solution.py:407
Async XLA Ops:
  0.6 1.3 %copy-start = (bf16[27,96,96]{2,1,0:T(8,128)(2,1)S(1)}, bf16[27,96,96]{2,1,0:T(8,128)(2,1)}, u32[]{:S(2)}) copy-start(bf16[27,96,96]{2,1,0:T(8,128)(2,1)} %w_ref.1) | copy-start | bytes 1492996
  1.7 0.7 %copy-start.1 = (bf16[48]{0:T(256)(128)(2,1)S(1)}, bf16[48]{0:T(256)(128)(2,1)}, u32[]{:S(2)}) copy-start(bf16[48]{0:T(256)(128)(2,1)} %param.6) | copy-start | bytes 292

commit v3 on v2

--- a/solution.py
+++ b/solution.py
@@ -48,6 +48,7 @@
     pix = x_ref.shape[2]
     full = 2 * own
     chunk = pack.shape[0] // n
+    half_chunk = chunk // 2
     me = lax.axis_index("tm")
     ch = lax.axis_index("chan")
     other = 1 - ch
@@ -213,7 +214,7 @@
     x_arrived(1)
     y[1] += dot(w_early[:, 0:full], xe[full : 2 * full, :])
     bias_sum = activate(1, lambda: x_forward(0))
-    product = dot_nt(g9[1], xe[full : 4 * full, :])
+    product_late = dot_nt(g9[1], xe[full : 4 * full, :])
     x_arrived(0)
     y[0] += dot(w_early[...], xe[0 : 2 * full, :])
     bias_sum += activate(0, lambda: None)
@@ -221,64 +222,70 @@
     rest = 3 * full - 256
     piece = 112
     base = 2 * taps
-    product += dot_nt(g9[0], xe[0 : 3 * full, :])
-    pack[0:taps, :] = product[:, 0:128].astype(BF16)
-    pack[taps:base, :] = product[:, 128:256].astype(BF16)
-    if pack.shape[0] > base:
-        pack[base:, :] = jnp.zeros((pack.shape[0] - base, 128), BF16)
+    middle = n * chunk // 2
+
+    def part(h, i):
+        return pl.ds(pl.multiple_of(h * middle + i * half_chunk, 16), half_chunk)
+
+    def rs_copy(h, d):
+        to = lax.rem(me + d, n)
+        return pltpu.make_async_remote_copy(
+            src_ref=pack.at[part(h, to)],
+            dst_ref=parts.at[h, d],
+            send_sem=rs_send.at[h, d],
+            recv_sem=rs_recv.at[h, d],
+            device_id=(to, ch),
+            device_id_type=MESH,
+        )
+
+    def ag_copy(h, d):
+        return pltpu.make_async_remote_copy(
+            src_ref=whole.at[part(h, me)],
+            dst_ref=whole.at[part(h, me)],
+            send_sem=ag_send.at[h, d],
+            recv_sem=ag_recv.at[h, d],
+            device_id=(lax.rem(me + d, n), ch),
+            device_id_type=MESH,
+        )
+
+    def ag_arrival(h, d):
+        come = part(h, lax.rem(me + n - d, n))
+        return pltpu.make_async_remote_copy(
+            src_ref=whole.at[come],
+            dst_ref=whole.at[come],
+            send_sem=ag_send.at[h, d],
+            recv_sem=ag_recv.at[h, d],
+            device_id=(lax.rem(me + d, n), ch),
+            device_id_type=MESH,
+        )
+
+    def each(act):
+        def step(d, carry):
+            act(d)
+            return carry
+
+        lax.fori_loop(1, n, step, 0)
+
+    wide = product_late[:, 0:256] + dot_nt(g9[0], xe[0:256, :])
+    pack[0:taps, :] = wide[:, 0:128].astype(BF16)
+    pack[taps:base, :] = wide[:, 128:256].astype(BF16)
+    early_start = middle <= base
+    if early_start:
+        each(lambda d: rs_copy(0, d).start())
+    narrow = product_late[:, 256:] + dot_nt(g9[0], xe[256 : 3 * full, :])
+    pack[base:, :] = jnp.zeros((pack.shape[0] - base, 128), BF16)
     for k in range(4):
         stop = min(taps, (k + 1) * piece)
-        pack[base : base + stop - k * piece, rest * k : rest * (k + 1)] = product[
-            k * piece : stop, 256 : 256 + rest
+        pack[base : base + stop - k * piece, rest * k : rest * (k + 1)] = narrow[
+            k * piece : stop, :
         ].astype(BF16)
     lane = lax.broadcasted_iota(jnp.int32, (own, 128), 1)
     pack[base + piece : base + piece + own, :] = jnp.where(
         lane == 0, jnp.broadcast_to(bias_sum, (own, 128)), 0.0
     ).astype(BF16)
-
-    def part(i):
-        return pl.ds(pl.multiple_of(i * chunk, 16), chunk)
-
-    def rs_copy(d):
-        to = lax.rem(me + d, n)
-        return pltpu.make_async_remote_copy(
-            src_ref=pack.at[part(to)],
-            dst_ref=parts.at[d],
-            send_sem=rs_send.at[d],
-            recv_sem=rs_recv.at[d],
-            device_id=(to, ch),
-            device_id_type=MESH,
-        )
-
-    def ag_copy(d):
-        return pltpu.make_async_remote_copy(
-            src_ref=whole.at[part(me)],
-            dst_ref=whole.at[part(me)],
-            send_sem=ag_send.at[d],
-            recv_sem=ag_recv.at[d],
-            device_id=(lax.rem(me + d, n), ch),
-            device_id_type=MESH,
-        )
-
-    def ag_arrival(d):
-        come = part(lax.rem(me + n - d, n))
-        return pltpu.make_async_remote_copy(
-            src_ref=whole.at[come],
-            dst_ref=whole.at[come],
-            send_sem=ag_send.at[d],
-            recv_sem=ag_recv.at[d],
-            device_id=(lax.rem(me + d, n), ch),
-            device_id_type=MESH,
-        )
-
-    def each(act):
-        def step(d, carry):
-            act(d)
-            return carry
-
-        lax.fori_loop(1, n, step, 0)
-
-    each(lambda d: rs_copy(d).start())
+    if not early_start:
+        each(lambda d: rs_copy(0, d).start())
+    each(lambda d: rs_copy(1, d).start())
 
     g_share(1).wait_recv()
     g_share(0).wait_recv()
@@ -292,13 +299,15 @@
             g_halo(f).wait_recv()
             g_relay(f).start()
 
-    def add_part(d, total):
-        rs_copy(d).wait_recv()
-        return total + parts[d].astype(F32)
-
-    total = lax.fori_loop(1, n, add_part, pack[part(me), :].astype(F32))
-    whole[part(me), :] = total.astype(BF16)
-    each(lambda d: ag_copy(d).start())
+    for h in range(2):
+
+        def add_part(d, total):
+            rs_copy(h, d).wait_recv()
+            return total + parts[h, d].astype(F32)
+
+        total = lax.fori_loop(1, n, add_part, pack[part(h, me), :].astype(F32))
+        whole[part(h, me), :] = total.astype(BF16)
+        each(lambda d: ag_copy(h, d).start())
 
     @pl.when(jnp.logical_not(last))
     def _():
@@ -315,7 +324,8 @@
         for block in range(0, own, 16):
             gin_ref[f, block : block + 16, :] = spatial_sum(f, block, 16, -1).astype(BF16)
 
-    each(lambda d: ag_arrival(d).wait_recv())
+    for h in range(2):
+        each(lambda d: ag_arrival(h, d).wait_recv())
     for f in range(2):
         x_share(f).wait_send()
         g_share(f).wait_send()
@@ -332,8 +342,9 @@
             g_halo(f).wait_send()
             x_relay(f).wait_send()
 
-    each(lambda d: rs_copy(d).wait_send())
-    each(lambda d: ag_copy(d).wait_send())
+    for h in range(2):
+        each(lambda d: rs_copy(h, d).wait_send())
+        each(lambda d: ag_copy(h, d).wait_send())
 
 
 def unpack(norm, own, full, whole, gw_ref, gb_ref):
@@ -369,7 +380,7 @@
     full = weight.shape[1]
     norm = 1.0 / math.sqrt(frames * n * pix)
     need = 2 * 9 * own + 112 + own
-    chunk = -(-need // (16 * n)) * 16
+    chunk = -(-need // (32 * n)) * 32
     vmem = pl.BlockSpec(memory_space=pltpu.VMEM)
     dma = pltpu.SemaphoreType.DMA
     out, gin, packed = pl.pallas_call(
@@ -391,9 +402,9 @@
             pltpu.VMEM((2, 9 * own, pix), F32),
             pltpu.VMEM((2, 9 * own, pix), BF16),
             pltpu.VMEM((n * chunk, 128), BF16),
-            pltpu.VMEM((n, chunk, 128), BF16),
+            pltpu.VMEM((2, n, chunk // 2, 128), BF16),
             dma((6,)), dma((6,)), dma((6,)), dma((6,)),
-            dma((n,)), dma((n,)), dma((n,)), dma((n,)),
+            dma((2, n)), dma((2, n)), dma((2, n)), dma((2, n)),
         ],
         compiler_params=pltpu.CompilerParams(
             collective_id=0, has_side_effects=True, vmem_limit_bytes=48 * 1024 * 1024

time: 36.9 us -> 39.2 us (1.062)
  Pallas kernels: 32.7 us -> 35 us
    pallas_call x1, Pallas kernels: 31.5 us -> 33.8 us  [local(): pl.pallas_call(functools.partial(kernel, n), out_shape=(jax.ShapeDtypeStr...]
where the time goes in v3:
time: 39.2 us; the launch traced here: 39 us
  Pallas kernels  35 us (89%)
  local copies, waits for them, and re-layouts  3.39 us (9%)
  between operations  0.66 us (2%)
    pallas_call x1, Pallas kernels, local(): pl.pallas_call(functools.partial(kernel, n), out_shape=(jax.ShapeDtypeStr...  33.8 us
    unnamed x6, local copies, waits for them, and re-layouts  2.29 us
    pallas_call x1, Pallas kernels, local(): pl.pallas_call(functools.partial(unpack, norm, own, full), out_shape=(jax...  1.16 us
    transpose x1, local copies, waits for them, and re-layouts, local(): cotangent.transpose(1, 0, 2)  1.1 us

profile of v3, /device:TPU:0, one launch (start us, length us, event | category | flops | bytes accessed | tf_op | source)
XLA Modules:
  0.0 39.0 jit_solution(2769438429679984205)
XLA Ops:
  0.6 0.0 copy-start
  0.6 1.1 %copy_bitcast_fusion = (bf16[2,48,896]{2,1,0:T(8,128)(2,1)S(1)}, bf16[2,48,896]{2,1,0:T(8,128)(2,1)S(1)}) fusion(bf16[48,2,896]{2,1,0:T(2,128)(2,1)} %param.7, bf16[48,2,896]{2,1,0:T(2,128)(2,1)} %param.4), kind=kLoop, calls=%fused_computation | loop fusion | bytes 688128 | tf_op jit(solution)/shard_map/transpose | solution.py:416
  1.7 0.0 copy-start.1
  1.8 0.1 copy-done
  1.9 0.6 %copy-done.1 = bf16[48]{0:T(256)(128)(2,1)S(1)} copy-done((bf16[48]{0:T(256)(128)(2,1)S(1)}, bf16[48]{0:T(256)(128)(2,1)}, u32[]{:S(2)}) %copy-start.1) | copy-done | bytes 120
  2.4 33.8 %shard_map.75 = (bf16[2,48,896]{2,1,0:T(8,128)(2,1)S(1)}, bf16[2,48,896]{2,1,0:T(8,128)(2,1)S(1)}, bf16[1024,128]{1,0:T(8,128)(2,1)S(1)}) custom-call(bf16[2,48,896]{2,1,0:T(8,128)(2,1)S(1)} %get-tuple-element.19.x_ref, bf16[27,96,96]{2,1,0:T(8,128)(2,1)S(1)} %copy-done, bf16[1,48]{1,0:T(2,128)(2,1)S(1)} %bitcast.10, ...), custom_call_target="tpu_custom_call" | custom-call | tf_op jit(solution)/shard_map/pallas_call | solution.py:386
  36.2 0.8 %copy.10 = bf16[48,2,896]{2,1,0:T(2,128)(2,1)} copy(bf16[48,2,896]{2,0,1:T(8,128)(2,1)S(1)} %bitcast.9) | data formatting | bytes 344064
  37.0 0.8 %copy.11 = bf16[48,2,896]{2,1,0:T(2,128)(2,1)} copy(bf16[48,2,896]{2,0,1:T(8,128)(2,1)S(1)} %bitcast.8) | data formatting | bytes 344064
  37.9 1.2 %shard_map.76 = (f32[27,48,96]{2,1,0:T(8,128)}, f32[1,48]{1,0:T(1,128)}) custom-call(bf16[1024,128]{1,0:T(8,128)(2,1)S(1)} %get-tuple-element.11.whole), custom_call_target="tpu_custom_call" | custom-call | tf_op jit(solution)/shard_map/pallas_call | solution.py:418
Async XLA Ops:
  0.6 1.3 %copy-start = (bf16[27,96,96]{2,1,0:T(8,128)(2,1)S(1)}, bf16[27,96,96]{2,1,0:T(8,128)(2,1)}, u32[]{:S(2)}) copy-start(bf16[27,96,96]{2,1,0:T(8,128)(2,1)} %w_ref.1) | copy-start | bytes 1492996
  1.7 0.7 %copy-start.1 = (bf16[48]{0:T(256)(128)(2,1)S(1)}, bf16[48]{0:T(256)(128)(2,1)}, u32[]{:S(2)}) copy-start(bf16[48]{0:T(256)(128)(2,1)} %param.6) | copy-start | bytes 292
